TPU v7x, 256 devices: a whole 4x4x8 slice. The times are simulated.
256 devices in a mesh: section: 16 (over y, z_lo), tensor: 16 (over z_hi, x, core).
Axes of the slice: x: 4, y: 4, z: 8 (z_hi: 2, z_lo: 4; z = z_hi * 4 + z_lo), core: 2. Of those that a mesh axis runs over, the one named last changes fastest.
Arguments:
- heads_out: bfloat16 [16, 1024, 6144], P('section', None, 'tensor'), may hold values from -6 to 6
- projection: bfloat16 [16, 6144, 6144], P('section', 'tensor'), may hold values from -0.078125 to 0.078125
- incoming: bfloat16 [16, 1024, 6144], P('section', 'tensor'), may hold values from -6 to 6
- parked: bfloat16 [16, 1024, 6144], P('section', None, 'tensor'), may hold values from -0.1875 to 0.1875
Outputs:
- activation: bfloat16 [16, 1024, 6144], P('section', 'tensor')
- heads_gradient: bfloat16 [16, 1024, 6144], P('section', None, 'tensor')
- weight_gradient: bfloat16 [16, 6144, 6144], P('section', 'tensor')
All inputs are finite; a program needn't handle non-finite values.
Results may differ from a plain program's by a relative error of at most 0.018.
Values may be sent and summed in bfloat16 or wider, within the bound.
A program may use at most 128 MiB of HBM per device.

v0:
```python
import jax
import jax.numpy as jnp
from jax import lax
from jax.sharding import PartitionSpec as P

feature_axes = (((1,), (1,)), ((), ()))
token_axes = (((0,), (0,)), ((), ()))


def passed_along(value, axis, steps):
    count = lax.axis_size(axis)
    pairs = [(source, (source + steps) % count) for source in range(count)]
    return lax.ppermute(value, axis, pairs)


def forward_pass(heads_out, weight):
    whole_term = jnp.dot(heads_out, weight, preferred_element_type=jnp.float32)
    summed = lax.psum_scatter(
        whole_term.astype(jnp.bfloat16), "tensor", scatter_dimension=0, tiled=True
    )
    return passed_along(summed[None], "section", 1)


def backward_pass(incoming, parked, weight):
    upstream = passed_along(incoming, "section", -1)[0]
    stored = passed_along(parked, "section", lax.axis_size("section") // 2)[0]
    gathered = lax.all_gather(upstream, "tensor", axis=0, tiled=True)
    heads_grad = lax.dot_general(gathered, weight, feature_axes, preferred_element_type=jnp.float32)
    weight_grad = lax.dot_general(stored, gathered, token_axes, preferred_element_type=jnp.float32)
    return (heads_grad.astype(jnp.bfloat16)[None], weight_grad.astype(jnp.bfloat16)[None])


def shards(heads_out, projection, incoming, parked):
    weight = projection[0]
    activation = forward_pass(heads_out[0], weight)
    heads_gradient, weight_gradient = backward_pass(incoming, parked, weight)
    return (activation, heads_gradient, weight_gradient)


def solution(mesh):
    return jax.shard_map(
        shards,
        mesh=mesh,
        in_specs=(
            P("section", None, "tensor"),
            P("section", "tensor", None),
            P("section", "tensor", None),
            P("section", None, "tensor"),
        ),
        out_specs=(
            P("section", "tensor", None),
            P("section", None, "tensor"),
            P("section", "tensor", None),
        ),
        check_vma=False,
    )
```

profile of v0, /device:TPU:1, one launch (start us, length us, event | category | flops | bytes accessed | tf_op | source)
XLA Modules:
  0.0 371.1 jit_solution(16780377304974940925)
XLA Ops:
  7.2 0.0 copy-start
  7.2 0.0 reduce-scatter.2.cloned.1.call-start
  7.2 1.1 copy-done
  8.3 11.8 %convolution_convert_fusion = bf16[1024,6144]{1,0:T(8,128)(2,1)} fusion(bf16[1,384,6144]{2,1,0:T(8,128)(2,1)} %param.5, bf16[1,1024,384]{2,1,0:T(8,128)(2,1)S(1)} %copy-done), kind=kOutput, calls=%fused_computation.4 | convolution fusion | flops 4838129664 | bytes 18087936 | tf_op jit(solution)/shard_map/dot_general | solution.py:17
  20.1 0.0 copy-start.3
  20.1 0.0 copy-start.4
  20.1 0.0 reduce-scatter.2.cloned.1.call-update
  20.1 0.0 all-gather.3.cloned.1.call-start
  20.2 1.1 copy-done.3
  21.2 7.6 %collective-permute-start.1 = (bf16[1,64,6144]{2,1,0:T(8,128)(2,1)S(1)}, bf16[1,64,6144]{2,1,0:T(8,128)(2,1)S(1)}, u32[]{:S(2)}, u32[]{:S(2)}) collective-permute-start(bf16[1,64,6144]{2,1,0:T(8,128)(2,1)S(1)} %copy-done.3), channel_id=1, source_target_pairs={{0,240},{16,0},{32,16},{48,32},{64,48},{80,64},{96,80},{112,96},{1... | collective-permute-start | bytes 2359304 | tf_op jit(solution)/shard_map/ppermute | solution.py:13
  28.9 16.2 %collective-permute-done.1 = bf16[1,64,6144]{2,1,0:T(8,128)(2,1)S(1)} collective-permute-done((bf16[1,64,6144]{2,1,0:T(8,128)(2,1)S(1)}, bf16[1,64,6144]{2,1,0:T(8,128)(2,1)S(1)}, u32[]{:S(2)}, u32[]{:S(2)}) %collective-permute-start.1) | collective-permute-done | bytes 786464 | tf_op jit(solution)/shard_map/ppermute | solution.py:13
  45.1 0.0 copy-start.2
  45.1 0.9 copy-done.2
  46.0 0.0 all-gather.3.cloned.1.call-update
  46.0 153.3 %reduce-scatter.2.cloned.1.call-done = bf16[64,6144]{1,0:T(8,128)(2,1)} async-done(((bf16[1024,6144]{1,0:T(8,128)(2,1)}), bf16[64,6144]{1,0:T(8,128)(2,1)}) %reduce-scatter.2.cloned.1.call-update) | async-done | bytes 786448 | tf_op jit(solution)/shard_map/reduce_scatter | solution.py:18
  199.2 1.9 collective-permute-start
  201.1 0.0 copy-done.4
  201.1 2.7 collective-permute-start.2
  203.9 17.2 %collective-permute-done = bf16[1,64,6144]{2,1,0:T(8,128)(2,1)S(1)} collective-permute-done((bf16[1,64,6144]{2,1,0:T(8,128)(2,1)}, bf16[1,64,6144]{2,1,0:T(8,128)(2,1)S(1)}, u32[]{:S(2)}, u32[]{:S(2)}) %collective-permute-start) | collective-permute-done | bytes 786464 | tf_op jit(solution)/shard_map/ppermute | solution.py:13
  221.1 123.6 %all-gather.3.cloned.1.call-done = bf16[1,1024,6144]{2,1,0:T(8,128)(2,1)} async-done(((bf16[1,64,6144]{2,1,0:T(8,128)(2,1)}), bf16[1,1024,6144]{2,1,0:T(8,128)(2,1)}) %all-gather.3.cloned.1.call-update) | async-done | bytes 12582928 | tf_op jit(solution)/shard_map/all_gather | solution.py:27
  344.7 0.0 copy-start.1
  344.7 11.9 %fusion.17 = bf16[1,1024,384]{2,1,0:T(8,128)(2,1)} fusion(bf16[1,384,6144]{2,1,0:T(8,128)(2,1)} %param.5, bf16[1,1024,6144]{2,1,0:T(8,128)(2,1)} %all-gather.3.cloned.1.call-done), kind=kOutput, calls=%fused_computation.10 | convolution fusion | flops 4832231424 | bytes 18087936 | tf_op jit(solution)/shard_map/dot_general | solution.py:28
  356.7 0.0 collective-permute-done.2
  356.7 0.0 copy-done.1
  356.7 6.7 %fusion.7 = bf16[1,384,6144]{2,1,0:T(8,128)(2,1)} fusion(bf16[1,1024,6144]{2,1,0:T(8,128)(2,1)S(1)} %copy-done.1, bf16[1,1024,384]{2,1,0:T(8,128)(2,1)S(1)} %collective-permute-done.2), kind=kOutput, calls=%fused_computation.6 | convolution fusion | flops 4834197504 | bytes 18087936 | tf_op jit(solution)/shard_map/dot_general | solution.py:29
  363.4 0.9 copy.8
Async XLA Ops:
  7.2 1.1 copy-start
  7.2 192.1 %reduce-scatter.2.cloned.1.call-start = ((), (), s32[]{:S(2)}) async-start(), calls=%async_computation.1 | async-start | bytes 13369344 | tf_op jit(solution)/shard_map/reduce_scatter | solution.py:18
  20.1 1.1 copy-start.3
  20.1 181.0 %copy-start.4 = (bf16[1,1024,384]{2,1,0:T(8,128)(2,1)S(1)}, bf16[1,1024,384]{2,1,0:T(8,128)(2,1)}, u32[]{:S(2)}) copy-start(bf16[1,1024,384]{2,1,0:T(8,128)(2,1)} %param.7) | copy-start | bytes 2359300
  20.1 324.6 %all-gather.3.cloned.1.call-start = ((), (), s32[]{:S(2)}) async-start(), calls=%async_computation.2 | async-start | bytes 13369344 | tf_op jit(solution)/shard_map/all_gather | solution.py:27
  21.2 23.8 %collective-permute-start.1 = (bf16[1,64,6144]{2,1,0:T(8,128)(2,1)S(1)}, bf16[1,64,6144]{2,1,0:T(8,128)(2,1)S(1)}, u32[]{:S(2)}, u32[]{:S(2)}) collective-permute-start(bf16[1,64,6144]{2,1,0:T(8,128)(2,1)S(1)} %copy-done.3), channel_id=1, source_target_pairs={{0,240},{16,0},{32,16},{48,32},{64,48},{80,64},{96,80},{112,96},{1... | collective-permute-start | bytes 2359304 | tf_op jit(solution)/shard_map/ppermute | solution.py:13
  45.1 0.9 copy-start.2
  199.2 21.9 %collective-permute-start = (bf16[1,64,6144]{2,1,0:T(8,128)(2,1)}, bf16[1,64,6144]{2,1,0:T(8,128)(2,1)S(1)}, u32[]{:S(2)}, u32[]{:S(2)}) collective-permute-start(bf16[1,64,6144]{2,1,0:T(8,128)(2,1)} %bitcast.33), channel_id=1, source_target_pairs={{0,16},{16,32},{32,48},{48,64},{64,80},{80,96},{96,112},{112,128},... | collective-permute-start | bytes 2359304 | tf_op jit(solution)/shard_map/ppermute | solution.py:13
  201.1 155.5 %collective-permute-start.2 = (bf16[1,1024,384]{2,1,0:T(8,128)(2,1)S(1)}, bf16[1,1024,384]{2,1,0:T(8,128)(2,1)S(1)}, u32[]{:S(2)}, u32[]{:S(2)}) collective-permute-start(bf16[1,1024,384]{2,1,0:T(8,128)(2,1)S(1)} %copy-done.4), channel_id=1, source_target_pairs={{0,128},{16,144},{32,160},{48,176},{64,192},{80,208},{96,224},{112... | collective-permute-start | bytes 2359304 | tf_op jit(solution)/shard_map/ppermute | solution.py:13
  344.7 11.9 %copy-start.1 = (bf16[1,1024,6144]{2,1,0:T(8,128)(2,1)S(1)}, bf16[1,1024,6144]{2,1,0:T(8,128)(2,1)}, u32[]{:S(2)}) copy-start(bf16[1,1024,6144]{2,1,0:T(8,128)(2,1)} %all-gather.3.cloned.1.call-done) | copy-start | bytes 37748740
Sparse Core Ops, SparseCore 0:
  20.3 178.9 reduce-scatter.1
  202.9 141.7 all-gather.2
where the time goes:
time: 371 us
  waiting for transfers between devices  310 us (84%)
  matrix products  30.5 us (8%)
  between operations  14.1 us (4%)
  starting transfers between devices  12.3 us (3%)
  local copies, waits for them, and re-layouts  3.91 us (1%)
    reduce_scatter x1, waiting for transfers between devices, forward_pass(): lax.psum_scatter(whole_term.astype(jnp.bfloat16), 'tensor', scatter_dimen...  153 us
    all_gather x1, waiting for transfers between devices, backward_pass(): gathered = lax.all_gather(upstream, 'tensor', axis=0, tiled=True)  124 us
    ppermute x3, waiting for transfers between devices, passed_along(): return lax.ppermute(value, axis, pairs)  33.4 us
    ppermute x3, starting transfers between devices, passed_along(): return lax.ppermute(value, axis, pairs)  12.2 us
    dot_general x1, matrix products, backward_pass(): lax.dot_general(gathered, weight, feature_axes, preferred_element_type=jn...  11.9 us
    dot_general x1, matrix products, forward_pass(): whole_term = jnp.dot(heads_out, weight, preferred_element_type=jnp.float32)  11.8 us
  transfers between devices with their start and end apart: 5, of which 4 were waited for; matrix products, arithmetic and copies ran while one was open for 3% of the time, Pallas kernels for 0%

commit v1 on v0

v1 whole, which is shorter than its diff:
```python
import functools

import jax
import jax.numpy as jnp
from jax import lax
from jax.experimental import pallas as pl
from jax.experimental.pallas import tpu as pltpu
from jax.sharding import PartitionSpec as P

MESH = pl.DeviceIdType.MESH
CHUNKS = 12
ROWS = 64
STAGES = {
    "share": 0,
    "combine": 1,
    "relay": 3,
    "reduce": 5,
    "spread": 7,
    "forward": 9,
    "pair": 11,
    "multiply": 12,
    "finish": 13,
}
TURN_AT = 8
feature_axes = (((1,), (1,)), ((), ()))


def matmul(a, b):
    return jnp.dot(a, b, preferred_element_type=jnp.float32)


def wait_bytes(ref, sem):
    pltpu.make_async_copy(ref, ref, sem).wait()


def kernel(
    heads, weight, incoming, parked,
    activation, heads_gradient, weight_gradient,
    heads_v, weight_v, stored_v, turned_v, up_v, half_v, half_in, sums, relay_in, direct_in, final_in,
    total, heads_out_v, weight_out_v, act_v,
    load_sem, weight_sem, out_sem, send_sem, near_sem, far_sem, left_sem, right_sem, rest_sem, pair_sem,
    share_sem, relay_sem, direct_sem, final_sem, stored_sem,
):
    width = weight_v.shape[2]
    half = heads_v.shape[1]
    section, tensor = lax.axis_index("section"), lax.axis_index("tensor")
    z_lo, z_hi, x, core = section % 4, tensor // 8, (tensor // 2) % 4, tensor % 2
    z = z_hi * 4 + z_lo
    right, left, across = (x + 1) % 4, (x + 3) % 4, (x + 2) % 4
    above, below = (section + 1) % 16, (section + 15) % 16
    up_hi, down_hi = ((z + 1) % 8) // 4, ((z + 7) % 8) // 4

    def member(hi, column):
        return hi * 8 + column * 2 + core

    sibling = (section, tensor + 1 - 2 * core)
    to_right, to_left = (section, member(z_hi, right)), (section, member(z_hi, left))
    near_up, far_up = (above, member(up_hi, x)), (above, member(1 - up_hi, x))
    near_down, far_down = (below, member(down_hi, x)), (below, member(1 - down_hi, x))
    opposite = ((section + 8) % 16, tensor)

    def rows_of(hi, column):
        return pl.ds(pl.multiple_of(core * half + (hi * 4 + column) * ROWS, ROWS), ROWS)

    def own_half():
        return pl.ds(pl.multiple_of(core * half, half), half)

    def send(src, dst, stage, recv, device):
        pltpu.make_async_remote_copy(
            src_ref=src, dst_ref=dst, send_sem=send_sem.at[stage], recv_sem=recv, device_id=device, device_id_type=MESH
        ).start()

    def columns(j):
        return pl.ds(pl.multiple_of(j * width, width), width)

    def load_heads(slot, colour):
        return pltpu.make_async_copy(heads.at[:, colour], heads_v.at[slot].reshape(8, ROWS, heads_v.shape[2]), load_sem.at[slot])

    def load_weight(j):
        return pltpu.make_async_copy(weight.at[:, columns(j)], weight_v.at[j], weight_sem.at[j])

    load_heads(1, 1 - core).start()
    load_weight(0).start()
    load_heads(0, core).start()

    @pl.loop(1, CHUNKS)
    def _(j):
        load_weight(j).start()

    barrier = pltpu.get_barrier_semaphore()
    peers = (sibling, to_right, to_left, near_up, far_up, near_down, far_down, opposite)
    for peer in peers:
        pl.semaphore_signal(barrier, inc=1, device_id=peer, device_id_type=MESH)
    pl.semaphore_wait(barrier, len(peers))

    @pl.loop(0, CHUNKS)
    def _(j):
        own = rows_of(z_hi, x)
        send(incoming.at[:, columns(j)], up_v.at[j, own], 0, far_sem.at[j], far_down)
        send(incoming.at[:, columns(j)], up_v.at[j, own], 0, near_sem.at[j], near_down)

    for colour in range(2):
        send(parked.at[:, colour], stored_v.at[colour], 8, stored_sem, opposite)

    load_heads(1, 1 - core).wait()
    load_heads(0, core).wait()

    def share(j):
        load_weight(j).wait()
        half_v[j] = matmul(heads_v[1], weight_v[j]).astype(jnp.bfloat16)
        send(half_v.at[j], half_in.at[j], 1, share_sem.at[j], sibling)

    def combine(j):
        wait_bytes(half_in.at[j], share_sem.at[j])
        both = matmul(heads_v[0], weight_v[j]) + half_in[j].astype(jnp.float32)
        sums[j] = both.astype(jnp.bfloat16).reshape(2, 4, ROWS, width)
        send(sums.at[j, 0, across], relay_in.at[j, 0], 2, relay_sem.at[j, 0], to_right)
        send(sums.at[j, 1, across], relay_in.at[j, 1], 2, relay_sem.at[j, 1], to_left)
        send(sums.at[j, 1, right], direct_in.at[j, 0, 1], 2, direct_sem.at[j], to_right)
        send(sums.at[j, 0, left], direct_in.at[j, 1, 0], 2, direct_sem.at[j], to_left)

    def relay(j):
        for hi, column, device in ((0, right, to_right), (1, left, to_left)):
            wait_bytes(relay_in.at[j, hi], relay_sem.at[j, hi])
            added = sums[j, hi, column].astype(jnp.float32) + relay_in[j, hi].astype(jnp.float32)
            sums[j, hi, column] = added.astype(jnp.bfloat16)
            send(sums.at[j, hi, column], direct_in.at[j, hi, hi], 3, direct_sem.at[j], device)

    def reduce(j):
        wait_bytes(direct_in.at[j], direct_sem.at[j])
        for hi in range(2):
            added = sums[j, hi, x].astype(jnp.float32) + direct_in[j, 0, hi].astype(jnp.float32)
            sums[j, hi, x] = (added + direct_in[j, 1, hi].astype(jnp.float32)).astype(jnp.bfloat16)
        send(sums.at[j, 1 - up_hi, x], final_in.at[j, 1], 4, final_sem.at[j], far_up)
        send(sums.at[j, up_hi, x], final_in.at[j, 0], 4, final_sem.at[j], near_up)

    def finish(j):
        wait_bytes(final_in.at[j], final_sem.at[j])
        act_v[j] = (final_in[j, 0].astype(jnp.float32) + final_in[j, 1].astype(jnp.float32)).astype(jnp.bfloat16)
        pltpu.make_async_copy(act_v.at[j], activation.at[:, columns(j)], out_sem.at[0]).start()

    def spread(j):
        near, far = up_v.at[j, rows_of(up_hi, x)], up_v.at[j, rows_of(1 - up_hi, x)]
        wait_bytes(near, near_sem.at[j])
        send(near, near, 5, left_sem.at[j], to_right)
        send(near, near, 5, rest_sem.at[j], to_left)
        wait_bytes(far, far_sem.at[j])
        send(far, far, 5, right_sem.at[j], to_left)
        send(far, far, 5, rest_sem.at[j], to_right)

    def forward(j):
        near, far = up_v.at[j, rows_of(up_hi, left)], up_v.at[j, rows_of(1 - up_hi, right)]
        wait_bytes(near, left_sem.at[j])
        send(near, near, 6, rest_sem.at[j], to_right)
        wait_bytes(far, right_sem.at[j])
        send(far, far, 6, rest_sem.at[j], to_left)

    def pair(j):
        wait_bytes(up_v.at[j, pl.ds(0, 4 * ROWS)], rest_sem.at[j])
        mine = up_v.at[j, own_half()]
        send(mine, mine, 7, pair_sem.at[j], sibling)

    def turn():
        wait_bytes(stored_v, stored_sem)
        turned_v[...] = stored_v[...].reshape(2 * half, stored_v.shape[3]).T

    def multiply(j):
        wait_bytes(up_v.at[j, pl.ds(0, half)], pair_sem.at[j])
        block = up_v[j]
        term = lax.dot_general(block, weight_v[j], feature_axes, preferred_element_type=jnp.float32)

        @pl.when(j == 0)
        def _():
            total[...] = term

        @pl.when(j > 0)
        def _():
            total[...] += term

        @pl.when(j == CHUNKS - 1)
        def _():
            heads_out_v[...] = total[...].astype(jnp.bfloat16).reshape(heads_out_v.shape)
            for colour in range(2):
                pltpu.make_async_copy(heads_out_v.at[colour], heads_gradient.at[:, colour], out_sem.at[1]).start()

        weight_out_v[j] = matmul(turned_v[...], block).astype(jnp.bfloat16)
        pltpu.make_async_copy(weight_out_v.at[j], weight_gradient.at[:, columns(j)], out_sem.at[2]).start()

    stages = dict(
        share=share, combine=combine, relay=relay, reduce=reduce, spread=spread, forward=forward, pair=pair,
        multiply=multiply, finish=finish,
    )

    @pl.loop(0, CHUNKS + max(STAGES.values()))
    def _(i):
        for name, start in STAGES.items():
            pl.when((i >= start) & (i < start + CHUNKS))(functools.partial(stages[name], i - start))
        pl.when(i == TURN_AT)(turn)

    for stage, ref in ((0, final_in), (1, half_v), (2, direct_in), (3, final_in), (4, final_in), (5, direct_in), (6, final_in), (7, half_v), (8, stored_v)):
        wait_bytes(ref, send_sem.at[stage])
    wait_bytes(act_v, out_sem.at[0])
    wait_bytes(heads_out_v, out_sem.at[1])
    wait_bytes(weight_out_v, out_sem.at[2])


def section_step(heads_out, projection, incoming, parked):
    weight = projection[0]
    depth, model = weight.shape
    tokens = heads_out.shape[1]
    half, width = tokens // 2, model // CHUNKS
    blocked = (8, 2, ROWS, depth)
    bf16, f32 = jnp.bfloat16, jnp.float32
    dma = pltpu.SemaphoreType.DMA
    per_chunk = dma((CHUNKS,))
    outs = pl.pallas_call(
        kernel,
        out_shape=(
            jax.ShapeDtypeStruct((ROWS, model), bf16),
            jax.ShapeDtypeStruct(blocked, bf16),
            jax.ShapeDtypeStruct((depth, model), bf16),
        ),
        in_specs=[pl.BlockSpec(memory_space=pl.ANY)] * 4,
        out_specs=[pl.BlockSpec(memory_space=pl.ANY)] * 3,
        scratch_shapes=[
            pltpu.VMEM((2, half, depth), bf16),
            pltpu.VMEM((CHUNKS, depth, width), bf16),
            pltpu.VMEM((2, 8, ROWS, depth), bf16),
            pltpu.VMEM((depth, tokens), bf16),
            pltpu.VMEM((CHUNKS, tokens, width), bf16),
            pltpu.VMEM((CHUNKS, half, width), bf16),
            pltpu.VMEM((CHUNKS, half, width), bf16),
            pltpu.VMEM((CHUNKS, 2, 4, ROWS, width), bf16),
            pltpu.VMEM((CHUNKS, 2, ROWS, width), bf16),
            pltpu.VMEM((CHUNKS, 2, 2, ROWS, width), bf16),
            pltpu.VMEM((CHUNKS, 2, ROWS, width), bf16),
            pltpu.VMEM((tokens, depth), f32),
            pltpu.VMEM((2, 8, ROWS, depth), bf16),
            pltpu.VMEM((CHUNKS, depth, width), bf16),
            pltpu.VMEM((CHUNKS, ROWS, width), bf16),
            dma((2,)),
            per_chunk,
            dma((3,)),
            dma((9,)),
            per_chunk,
            per_chunk,
            per_chunk,
            per_chunk,
            per_chunk,
            per_chunk,
            per_chunk,
            dma((CHUNKS, 2)),
            per_chunk,
            per_chunk,
            dma,
        ],
        compiler_params=pltpu.CompilerParams(collective_id=0, has_side_effects=True, vmem_limit_bytes=62 << 20),
        cost_estimate=pl.CostEstimate(flops=6 * tokens * depth * model, bytes_accessed=14 << 20, transcendentals=0),
        name="relay_section",
    )(heads_out.reshape(blocked), weight, incoming[0], parked.reshape(blocked))
    activation, heads_gradient, weight_gradient = outs
    return activation[None], heads_gradient.reshape(1, tokens, depth), weight_gradient[None]


def solution(mesh):
    whole_tokens = P("section", None, "tensor")
    rows = P("section", "tensor", None)
    return jax.shard_map(
        section_step,
        mesh=mesh,
        in_specs=(whole_tokens, rows, rows, whole_tokens),
        out_specs=(rows, whole_tokens, rows),
        check_vma=False,
    )
```

time: 371 us -> 145 us (0.39)
  the two profiles are of different devices: /device:TPU:1 before, /device:TPU:121 now
where the time goes in v1:
time: 145 us
  Pallas kernels  135 us (93%)
  local copies, waits for them, and re-layouts  9.21 us (6%)
    pallas_call x1, Pallas kernels, section_step(): pl.pallas_call(kernel, out_shape=(jax.ShapeDtypeStruct((ROWS, model), bf1...  135 us
    unnamed x3, local copies, waits for them, and re-layouts  9.21 us

profile of v1, /device:TPU:121, one launch (start us, length us, event | category | flops | bytes accessed | tf_op | source)
XLA Modules:
  0.0 145.3 jit_solution(11502081139065042148)
XLA Ops:
  0.6 135.4 %relay_section.1 = (bf16[64,6144]{1,0:T(8,128)(2,1)}, bf16[8,2,64,384]{3,2,1,0:T(8,128)(2,1)}, bf16[384,6144]{1,0:T(8,128)(2,1)}) custom-call(bf16[8,2,64,384]{3,2,1,0:T(8,128)(2,1)} %bitcast.11, bf16[384,6144]{1,0:T(8,128)(2,1)} %bitcast.10, bf16[64,6144]{1,0:T(8,128)(2,1)} %bitcast.12, bf16[8,2,64,384]{3,2,1,0:T(8,128)(2,1)} %bitcast.13), custom_call_target="tpu_custom_call" | custom-call | flops 14495514624 | bytes 14680064 | tf_op jit(solution)/shard_map/relay_section/pallas_call | solution.py:216
  136.1 2.1 %copy.10 = bf16[1,64,6144]{2,1,0:T(8,128)(2,1)} copy(bf16[1,64,6144]{2,1,0:T(8,128)(2,1)} %bitcast.9) | data formatting | bytes 1572864
  138.1 2.1 %copy.11 = bf16[1,1024,384]{2,1,0:T(8,128)(2,1)} copy(bf16[1,1024,384]{2,1,0:T(8,128)(2,1)} %bitcast.8) | data formatting | bytes 1572864
  140.2 5.1 %copy.12 = bf16[1,384,6144]{2,1,0:T(8,128)(2,1)} copy(bf16[1,384,6144]{2,1,0:T(8,128)(2,1)} %bitcast.7) | data formatting | bytes 9437184

commit v2 on v1

--- a/solution.py
+++ b/solution.py
@@ -14,14 +14,17 @@
     "share": 0,
     "combine": 1,
     "relay": 3,
-    "reduce": 5,
-    "spread": 7,
-    "forward": 9,
-    "pair": 11,
-    "multiply": 12,
-    "finish": 13,
+    "reduce": 6,
+    "spread": 3,
+    "forward": 6,
+    "pair": 9,
+    "multiply": 10,
+    "finish": 12,
 }
-TURN_AT = 8
+CROSSED = 2
+CROSS = {"cross": 9, "pair": 13, "multiply": 14}
+FETCH_AT = 1
+TURN_AT = 9
 feature_axes = (((1,), (1,)), ((), ()))
 
 
@@ -35,11 +38,11 @@
 
 def kernel(
     heads, weight, incoming, parked,
-    activation, heads_gradient, weight_gradient,
+    act_v, heads_out_v, weight_out_v,
     heads_v, weight_v, stored_v, turned_v, up_v, half_v, half_in, sums, relay_in, direct_in, final_in,
-    total, heads_out_v, weight_out_v, act_v,
-    load_sem, weight_sem, out_sem, send_sem, near_sem, far_sem, left_sem, right_sem, rest_sem, pair_sem,
-    share_sem, relay_sem, direct_sem, final_sem, stored_sem,
+    total,
+    load_sem, weight_sem, send_sem, near_sem, far_sem, left_sem, right_sem, rest_sem, pair_sem,
+    share_sem, relay_sem, direct_sem, final_sem, stored_sem, cross_sem,
 ):
     width = weight_v.shape[2]
     half = heads_v.shape[1]
@@ -57,7 +60,7 @@
     to_right, to_left = (section, member(z_hi, right)), (section, member(z_hi, left))
     near_up, far_up = (above, member(up_hi, x)), (above, member(1 - up_hi, x))
     near_down, far_down = (below, member(down_hi, x)), (below, member(1 - down_hi, x))
-    opposite = ((section + 8) % 16, tensor)
+    opposite, partner = ((section + 8) % 16, tensor), (section, (tensor + 8) % 16)
 
     def rows_of(hi, column):
         return pl.ds(pl.multiple_of(core * half + (hi * 4 + column) * ROWS, ROWS), ROWS)
@@ -88,7 +91,7 @@
         load_weight(j).start()
 
     barrier = pltpu.get_barrier_semaphore()
-    peers = (sibling, to_right, to_left, near_up, far_up, near_down, far_down, opposite)
+    peers = (sibling, to_right, to_left, near_up, far_up, near_down, far_down, opposite, partner)
     for peer in peers:
         pl.semaphore_signal(barrier, inc=1, device_id=peer, device_id_type=MESH)
     pl.semaphore_wait(barrier, len(peers))
@@ -96,11 +99,11 @@
     @pl.loop(0, CHUNKS)
     def _(j):
         own = rows_of(z_hi, x)
-        send(incoming.at[:, columns(j)], up_v.at[j, own], 0, far_sem.at[j], far_down)
         send(incoming.at[:, columns(j)], up_v.at[j, own], 0, near_sem.at[j], near_down)
 
-    for colour in range(2):
-        send(parked.at[:, colour], stored_v.at[colour], 8, stored_sem, opposite)
+        @pl.when(j >= CROSSED)
+        def _():
+            send(incoming.at[:, columns(j)], up_v.at[j, own], 0, far_sem.at[j], far_down)
 
     load_heads(1, 1 - core).wait()
     load_heads(0, core).wait()
@@ -137,28 +140,49 @@
     def finish(j):
         wait_bytes(final_in.at[j], final_sem.at[j])
         act_v[j] = (final_in[j, 0].astype(jnp.float32) + final_in[j, 1].astype(jnp.float32)).astype(jnp.bfloat16)
-        pltpu.make_async_copy(act_v.at[j], activation.at[:, columns(j)], out_sem.at[0]).start()
 
     def spread(j):
         near, far = up_v.at[j, rows_of(up_hi, x)], up_v.at[j, rows_of(1 - up_hi, x)]
         wait_bytes(near, near_sem.at[j])
         send(near, near, 5, left_sem.at[j], to_right)
         send(near, near, 5, rest_sem.at[j], to_left)
-        wait_bytes(far, far_sem.at[j])
-        send(far, far, 5, right_sem.at[j], to_left)
-        send(far, far, 5, rest_sem.at[j], to_right)
+
+        @pl.when(j >= CROSSED)
+        def _():
+            wait_bytes(far, far_sem.at[j])
+            send(far, far, 5, right_sem.at[j], to_left)
+            send(far, far, 5, rest_sem.at[j], to_right)
 
     def forward(j):
         near, far = up_v.at[j, rows_of(up_hi, left)], up_v.at[j, rows_of(1 - up_hi, right)]
         wait_bytes(near, left_sem.at[j])
         send(near, near, 6, rest_sem.at[j], to_right)
-        wait_bytes(far, right_sem.at[j])
-        send(far, far, 6, rest_sem.at[j], to_left)
+
+        @pl.when(j >= CROSSED)
+        def _():
+            wait_bytes(far, right_sem.at[j])
+            send(far, far, 6, rest_sem.at[j], to_left)
+
+    def cross(j):
+        wait_bytes(up_v.at[j, pl.ds(0, 2 * ROWS)], rest_sem.at[j])
+        mine = up_v.at[j, pl.ds(pl.multiple_of(core * half + up_hi * 4 * ROWS, 4 * ROWS), 4 * ROWS)]
+        send(mine, mine, 9, cross_sem.at[j], partner)
 
     def pair(j):
-        wait_bytes(up_v.at[j, pl.ds(0, 4 * ROWS)], rest_sem.at[j])
+        @pl.when(j >= CROSSED)
+        def _():
+            wait_bytes(up_v.at[j, pl.ds(0, 4 * ROWS)], rest_sem.at[j])
+
+        @pl.when(j < CROSSED)
+        def _():
+            wait_bytes(up_v.at[j, pl.ds(0, 4 * ROWS)], cross_sem.at[j])
+
         mine = up_v.at[j, own_half()]
         send(mine, mine, 7, pair_sem.at[j], sibling)
+
+    def fetch_stored(block):
+        for colour in range(2):
+            send(parked.at[block, colour], stored_v.at[colour, block], 8, stored_sem, opposite)
 
     def turn():
         wait_bytes(stored_v, stored_sem)
@@ -169,39 +193,56 @@
         block = up_v[j]
         term = lax.dot_general(block, weight_v[j], feature_axes, preferred_element_type=jnp.float32)
 
-        @pl.when(j == 0)
-        def _():
-            total[...] = term
-
-        @pl.when(j > 0)
-        def _():
-            total[...] += term
-
-        @pl.when(j == CHUNKS - 1)
-        def _():
-            heads_out_v[...] = total[...].astype(jnp.bfloat16).reshape(heads_out_v.shape)
-            for colour in range(2):
-                pltpu.make_async_copy(heads_out_v.at[colour], heads_gradient.at[:, colour], out_sem.at[1]).start()
-
+        total[...] += term
         weight_out_v[j] = matmul(turned_v[...], block).astype(jnp.bfloat16)
-        pltpu.make_async_copy(weight_out_v.at[j], weight_gradient.at[:, columns(j)], out_sem.at[2]).start()
 
     stages = dict(
         share=share, combine=combine, relay=relay, reduce=reduce, spread=spread, forward=forward, pair=pair,
-        multiply=multiply, finish=finish,
+        multiply=multiply, finish=finish, cross=cross,
     )
+
+    total[...] = jnp.zeros_like(total)
 
     @pl.loop(0, CHUNKS + max(STAGES.values()))
     def _(i):
+        pl.when((i >= FETCH_AT) & (i < FETCH_AT + 8))(lambda: fetch_stored(i - FETCH_AT))
+        pl.when(i == TURN_AT)(turn)
         for name, start in STAGES.items():
-            pl.when((i >= start) & (i < start + CHUNKS))(functools.partial(stages[name], i - start))
-        pl.when(i == TURN_AT)(turn)
-
-    for stage, ref in ((0, final_in), (1, half_v), (2, direct_in), (3, final_in), (4, final_in), (5, direct_in), (6, final_in), (7, half_v), (8, stored_v)):
-        wait_bytes(ref, send_sem.at[stage])
-    wait_bytes(act_v, out_sem.at[0])
-    wait_bytes(heads_out_v, out_sem.at[1])
-    wait_bytes(weight_out_v, out_sem.at[2])
+            first = CROSSED if name in CROSS else 0
+            pl.when((i >= start + first) & (i < start + CHUNKS))(functools.partial(stages[name], i - start))
+        for name, start in CROSS.items():
+            pl.when((i >= start) & (i < start + CROSSED))(functools.partial(stages[name], i - start))
+
+    heads_out_v[...] = total[...].astype(jnp.bfloat16).reshape(heads_out_v.shape)
+    blocks = half_v.reshape(CHUNKS * 8, ROWS, width)
+    sent = {
+        0: 2 * CHUNKS - CROSSED,
+        1: 8 * CHUNKS,
+        2: 4 * CHUNKS,
+        3: 2 * CHUNKS,
+        4: 2 * CHUNKS,
+        5: 4 * CHUNKS - 2 * CROSSED,
+        6: 2 * CHUNKS - CROSSED,
+        7: 8 * CHUNKS,
+        9: 4 * CROSSED,
+    }
+    for stage, count in sent.items():
+        wait_bytes(blocks.at[pl.ds(0, count)], send_sem.at[stage])
+    wait_bytes(stored_v, send_sem.at[8])
+
+
+def publish(act_v, heads_out_v, weight_out_v, activation, heads_gradient, weight_gradient, sem):
+    width = act_v.shape[2]
+    copies = [pltpu.make_async_copy(heads_out_v.at[colour], heads_gradient.at[:, colour], sem.at[0]) for colour in range(2)]
+    for j in range(CHUNKS):
+        columns = pl.ds(j * width, width)
+        copies.append(pltpu.make_async_copy(weight_out_v.at[j], weight_gradient.at[:, columns], sem.at[1]))
+        copies.append(pltpu.make_async_copy(act_v.at[j], activation.at[:, columns], sem.at[2]))
+    for copy in copies:
+        copy.start()
+    wait_bytes(heads_out_v, sem.at[0])
+    wait_bytes(weight_out_v, sem.at[1])
+    wait_bytes(act_v, sem.at[2])
 
 
 def section_step(heads_out, projection, incoming, parked):
@@ -216,12 +257,12 @@
     outs = pl.pallas_call(
         kernel,
         out_shape=(
-            jax.ShapeDtypeStruct((ROWS, model), bf16),
-            jax.ShapeDtypeStruct(blocked, bf16),
-            jax.ShapeDtypeStruct((depth, model), bf16),
+            pltpu.VMEM((CHUNKS, ROWS, width), bf16),
+            pltpu.VMEM((2, 8, ROWS, depth), bf16),
+            pltpu.VMEM((CHUNKS, depth, width), bf16),
         ),
         in_specs=[pl.BlockSpec(memory_space=pl.ANY)] * 4,
-        out_specs=[pl.BlockSpec(memory_space=pl.ANY)] * 3,
+        out_specs=[pl.BlockSpec(memory_space=pltpu.VMEM)] * 3,
         scratch_shapes=[
             pltpu.VMEM((2, half, depth), bf16),
             pltpu.VMEM((CHUNKS, depth, width), bf16),
@@ -235,13 +276,9 @@
             pltpu.VMEM((CHUNKS, 2, 2, ROWS, width), bf16),
             pltpu.VMEM((CHUNKS, 2, ROWS, width), bf16),
             pltpu.VMEM((tokens, depth), f32),
-            pltpu.VMEM((2, 8, ROWS, depth), bf16),
-            pltpu.VMEM((CHUNKS, depth, width), bf16),
-            pltpu.VMEM((CHUNKS, ROWS, width), bf16),
             dma((2,)),
             per_chunk,
-            dma((3,)),
-            dma((9,)),
+            dma((10,)),
             per_chunk,
             per_chunk,
             per_chunk,
@@ -253,12 +290,25 @@
             per_chunk,
             per_chunk,
             dma,
+            per_chunk,
         ],
-        compiler_params=pltpu.CompilerParams(collective_id=0, has_side_effects=True, vmem_limit_bytes=62 << 20),
+        compiler_params=pltpu.CompilerParams(collective_id=0, has_side_effects=True, vmem_limit_bytes=52 << 20),
         cost_estimate=pl.CostEstimate(flops=6 * tokens * depth * model, bytes_accessed=14 << 20, transcendentals=0),
         name="relay_section",
     )(heads_out.reshape(blocked), weight, incoming[0], parked.reshape(blocked))
-    activation, heads_gradient, weight_gradient = outs
+    activation, heads_gradient, weight_gradient = pl.pallas_call(
+        publish,
+        out_shape=(
+            jax.ShapeDtypeStruct((ROWS, model), bf16),
+            jax.ShapeDtypeStruct(blocked, bf16),
+            jax.ShapeDtypeStruct((depth, model), bf16),
+        ),
+        in_specs=[pl.BlockSpec(memory_space=pltpu.VMEM)] * 3,
+        out_specs=[pl.BlockSpec(memory_space=pl.ANY)] * 3,
+        scratch_shapes=[dma((3,))],
+        compiler_params=pltpu.CompilerParams(vmem_limit_bytes=2 << 20),
+        name="publish",
+    )(*(pltpu.with_memory_space_constraint(out, pltpu.VMEM) for out in outs))
     return activation[None], heads_gradient.reshape(1, tokens, depth), weight_gradient[None]
 
 

time: 145 us -> 123 us (0.85)
  the two profiles are of different devices: /device:TPU:121 before, /device:TPU:1 now
where the time goes in v2:
time: 123 us
  Pallas kernels  122 us (99%)
    pallas_call x1, Pallas kernels, section_step(): pl.pallas_call(kernel, out_shape=(pltpu.VMEM((CHUNKS, ROWS, width), bf16)...  120 us
    pallas_call x1, Pallas kernels, section_step(): pl.pallas_call(publish, out_shape=(jax.ShapeDtypeStruct((ROWS, model), bf...  2.65 us

profile of v2, /device:TPU:1, one launch (start us, length us, event | category | flops | bytes accessed | tf_op | source)
XLA Modules:
  0.0 122.8 jit_solution(8576517140519699325)
XLA Ops:
  0.6 119.5 %relay_section.1 = (bf16[12,64,512]{2,1,0:T(8,128)(2,1)S(1)}, bf16[2,8,64,384]{3,2,1,0:T(8,128)(2,1)S(1)}, bf16[12,384,512]{2,1,0:T(8,128)(2,1)S(1)}) custom-call(bf16[8,2,64,384]{3,2,1,0:T(8,128)(2,1)} %bitcast.9, bf16[384,6144]{1,0:T(8,128)(2,1)} %bitcast.7, bf16[64,6144]{1,0:T(8,128)(2,1)} %bitcast.10, bf16[8,2,64,384]{3,2,1,0:T(8,128)(2,1)} %bitcast.11), custom_call_target="tpu_custom_call" | custom-call | flops 14495514624 | bytes 14680064 | tf_op jit(solution)/shard_map/relay_section/pallas_call | solution.py:257
  120.2 2.6 %publish.1 = (bf16[64,6144]{1,0:T(8,128)(2,1)}, bf16[8,2,64,384]{3,2,1,0:T(8,128)(2,1)}, bf16[384,6144]{1,0:T(8,128)(2,1)}) custom-call(bf16[12,64,512]{2,1,0:T(8,128)(2,1)S(1)} %get-tuple-element.9.act_v, bf16[2,8,64,384]{3,2,1,0:T(8,128)(2,1)S(1)} %get-tuple-element.10.heads_out_v, bf16[12,384,512]{2,1,0:T(8,128)(2,1)S(1)} %get-tuple-element.11.weight_out_v), custom_call_target="tpu_custom_call" | custom-call | tf_op jit(solution)/shard_map/publish/pallas_call | solution.py:299

commit v3 on v2

--- a/solution.py
+++ b/solution.py
@@ -11,20 +11,21 @@
 CHUNKS = 12
 ROWS = 64
 STAGES = {
-    "share": 0,
-    "combine": 1,
-    "relay": 3,
-    "reduce": 6,
-    "spread": 3,
-    "forward": 6,
-    "pair": 9,
-    "multiply": 10,
-    "finish": 12,
+    "launch": -4,
+    "share": -1,
+    "combine": 0,
+    "relay": 2,
+    "reduce": 4,
+    "spread": 2,
+    "forward": 4,
+    "pair": 6,
+    "multiply": 7,
+    "finish": 9,
 }
 CROSSED = 2
-CROSS = {"cross": 9, "pair": 13, "multiply": 14}
+CROSS = {"spread": -1, "cross": 7, "pair": 11, "multiply": 12}
 FETCH_AT = 1
-TURN_AT = 9
+TURN_AT = 8
 feature_axes = (((1,), (1,)), ((), ()))
 
 
@@ -38,9 +39,8 @@
 
 def kernel(
     heads, weight, incoming, parked,
-    act_v, heads_out_v, weight_out_v,
-    heads_v, weight_v, stored_v, turned_v, up_v, half_v, half_in, sums, relay_in, direct_in, final_in,
-    total,
+    act_v, total, turned_v, weight_out_v, block_v, last_weight_v,
+    heads_v, weight_v, stored_v, up_v, half_v, half_in, sums, relay_in, direct_in, final_in,
     load_sem, weight_sem, send_sem, near_sem, far_sem, left_sem, right_sem, rest_sem, pair_sem,
     share_sem, relay_sem, direct_sem, final_sem, stored_sem, cross_sem,
 ):
@@ -94,24 +94,25 @@
     peers = (sibling, to_right, to_left, near_up, far_up, near_down, far_down, opposite, partner)
     for peer in peers:
         pl.semaphore_signal(barrier, inc=1, device_id=peer, device_id_type=MESH)
-    pl.semaphore_wait(barrier, len(peers))
-
-    @pl.loop(0, CHUNKS)
-    def _(j):
+
+    def project(j):
+        load_weight(j).wait()
+        half_v[j] = matmul(heads_v[1], weight_v[j]).astype(jnp.bfloat16)
+
+    def send_half(j):
+        send(half_v.at[j], half_in.at[j], 1, share_sem.at[j], sibling)
+
+    def share(j):
+        project(j)
+        send_half(j)
+
+    def launch(j):
         own = rows_of(z_hi, x)
         send(incoming.at[:, columns(j)], up_v.at[j, own], 0, near_sem.at[j], near_down)
 
         @pl.when(j >= CROSSED)
         def _():
             send(incoming.at[:, columns(j)], up_v.at[j, own], 0, far_sem.at[j], far_down)
-
-    load_heads(1, 1 - core).wait()
-    load_heads(0, core).wait()
-
-    def share(j):
-        load_weight(j).wait()
-        half_v[j] = matmul(heads_v[1], weight_v[j]).astype(jnp.bfloat16)
-        send(half_v.at[j], half_in.at[j], 1, share_sem.at[j], sibling)
 
     def combine(j):
         wait_bytes(half_in.at[j], share_sem.at[j])
@@ -145,23 +146,32 @@
         near, far = up_v.at[j, rows_of(up_hi, x)], up_v.at[j, rows_of(1 - up_hi, x)]
         wait_bytes(near, near_sem.at[j])
         send(near, near, 5, left_sem.at[j], to_right)
-        send(near, near, 5, rest_sem.at[j], to_left)
+
+        @pl.when(j < CROSSED)
+        def _():
+            send(near, near, 5, rest_sem.at[j], to_left)
 
         @pl.when(j >= CROSSED)
         def _():
             wait_bytes(far, far_sem.at[j])
             send(far, far, 5, right_sem.at[j], to_left)
+
+    def forward(j):
+        near, far = up_v.at[j, rows_of(up_hi, x)], up_v.at[j, rows_of(1 - up_hi, x)]
+
+        @pl.when(j >= CROSSED)
+        def _():
+            send(near, near, 5, rest_sem.at[j], to_left)
             send(far, far, 5, rest_sem.at[j], to_right)
 
-    def forward(j):
-        near, far = up_v.at[j, rows_of(up_hi, left)], up_v.at[j, rows_of(1 - up_hi, right)]
-        wait_bytes(near, left_sem.at[j])
-        send(near, near, 6, rest_sem.at[j], to_right)
-
-        @pl.when(j >= CROSSED)
-        def _():
-            wait_bytes(far, right_sem.at[j])
-            send(far, far, 6, rest_sem.at[j], to_left)
+        passed_near, passed_far = up_v.at[j, rows_of(up_hi, left)], up_v.at[j, rows_of(1 - up_hi, right)]
+        wait_bytes(passed_near, left_sem.at[j])
+        send(passed_near, passed_near, 6, rest_sem.at[j], to_right)
+
+        @pl.when(j >= CROSSED)
+        def _():
+            wait_bytes(passed_far, right_sem.at[j])
+            send(passed_far, passed_far, 6, rest_sem.at[j], to_left)
 
     def cross(j):
         wait_bytes(up_v.at[j, pl.ds(0, 2 * ROWS)], rest_sem.at[j])
@@ -197,23 +207,34 @@
         weight_out_v[j] = matmul(turned_v[...], block).astype(jnp.bfloat16)
 
     stages = dict(
-        share=share, combine=combine, relay=relay, reduce=reduce, spread=spread, forward=forward, pair=pair,
+        launch=launch, share=share, combine=combine, relay=relay, reduce=reduce, spread=spread, forward=forward, pair=pair,
         multiply=multiply, finish=finish, cross=cross,
     )
 
+    load_heads(1, 1 - core).wait()
+    project(0)
+    pl.semaphore_wait(barrier, len(peers))
+    send_half(0)
+    pl.loop(0, -STAGES["launch"])(launch)
     total[...] = jnp.zeros_like(total)
+    load_heads(0, core).wait()
+    for j in range(-CROSS["spread"]):
+        spread(j)
 
     @pl.loop(0, CHUNKS + max(STAGES.values()))
     def _(i):
         pl.when((i >= FETCH_AT) & (i < FETCH_AT + 8))(lambda: fetch_stored(i - FETCH_AT))
         pl.when(i == TURN_AT)(turn)
         for name, start in STAGES.items():
-            first = CROSSED if name in CROSS else 0
-            pl.when((i >= start + first) & (i < start + CHUNKS))(functools.partial(stages[name], i - start))
+            first = CROSSED if name in CROSS else max(-start, 0)
+            count = CHUNKS - 1 if name == "multiply" else CHUNKS
+            pl.when((i >= start + first) & (i < start + count))(functools.partial(stages[name], i - start))
         for name, start in CROSS.items():
-            pl.when((i >= start) & (i < start + CROSSED))(functools.partial(stages[name], i - start))
-
-    heads_out_v[...] = total[...].astype(jnp.bfloat16).reshape(heads_out_v.shape)
+            pl.when((i >= max(start, 0)) & (i < start + CROSSED))(functools.partial(stages[name], i - start))
+
+    wait_bytes(up_v.at[CHUNKS - 1, pl.ds(0, half)], pair_sem.at[CHUNKS - 1])
+    block_v[...] = up_v[CHUNKS - 1]
+    last_weight_v[...] = weight_v[CHUNKS - 1]
     blocks = half_v.reshape(CHUNKS * 8, ROWS, width)
     sent = {
         0: 2 * CHUNKS - CROSSED,
@@ -231,18 +252,31 @@
     wait_bytes(stored_v, send_sem.at[8])
 
 
-def publish(act_v, heads_out_v, weight_out_v, activation, heads_gradient, weight_gradient, sem):
+def publish(
+    act_v, total, turned_v, weight_out_v, block_v, last_weight_v,
+    activation, heads_gradient, weight_gradient,
+    heads_out_v, last_v, sem,
+):
     width = act_v.shape[2]
-    copies = [pltpu.make_async_copy(heads_out_v.at[colour], heads_gradient.at[:, colour], sem.at[0]) for colour in range(2)]
+
+    def columns(j):
+        return pl.ds(j * width, width)
+
+    for j in range(CHUNKS - 1):
+        pltpu.make_async_copy(weight_out_v.at[j], weight_gradient.at[:, columns(j)], sem.at[0]).start()
     for j in range(CHUNKS):
-        columns = pl.ds(j * width, width)
-        copies.append(pltpu.make_async_copy(weight_out_v.at[j], weight_gradient.at[:, columns], sem.at[1]))
-        copies.append(pltpu.make_async_copy(act_v.at[j], activation.at[:, columns], sem.at[2]))
-    for copy in copies:
-        copy.start()
-    wait_bytes(heads_out_v, sem.at[0])
-    wait_bytes(weight_out_v, sem.at[1])
-    wait_bytes(act_v, sem.at[2])
+        pltpu.make_async_copy(act_v.at[j], activation.at[:, columns(j)], sem.at[1]).start()
+    block = block_v[...]
+    term = lax.dot_general(block, last_weight_v[...], feature_axes, preferred_element_type=jnp.float32)
+    heads_out_v[...] = (total[...] + term).astype(jnp.bfloat16).reshape(heads_out_v.shape)
+    for colour in range(2):
+        pltpu.make_async_copy(heads_out_v.at[colour], heads_gradient.at[:, colour], sem.at[2]).start()
+    last_v[...] = matmul(turned_v[...], block).astype(jnp.bfloat16)
+    pltpu.make_async_copy(last_v, weight_gradient.at[:, columns(CHUNKS - 1)], sem.at[3]).start()
+    wait_bytes(weight_out_v, sem.at[0])
+    wait_bytes(act_v, sem.at[1])
+    wait_bytes(heads_out_v, sem.at[2])
+    wait_bytes(last_v, sem.at[3])
 
 
 def section_step(heads_out, projection, incoming, parked):
@@ -258,16 +292,18 @@
         kernel,
         out_shape=(
             pltpu.VMEM((CHUNKS, ROWS, width), bf16),
-            pltpu.VMEM((2, 8, ROWS, depth), bf16),
-            pltpu.VMEM((CHUNKS, depth, width), bf16),
+            pltpu.VMEM((tokens, depth), f32),
+            pltpu.VMEM((depth, tokens), bf16),
+            pltpu.VMEM((CHUNKS - 1, depth, width), bf16),
+            pltpu.VMEM((tokens, width), bf16),
+            pltpu.VMEM((depth, width), bf16),
         ),
         in_specs=[pl.BlockSpec(memory_space=pl.ANY)] * 4,
-        out_specs=[pl.BlockSpec(memory_space=pltpu.VMEM)] * 3,
+        out_specs=[pl.BlockSpec(memory_space=pltpu.VMEM)] * 6,
         scratch_shapes=[
             pltpu.VMEM((2, half, depth), bf16),
             pltpu.VMEM((CHUNKS, depth, width), bf16),
             pltpu.VMEM((2, 8, ROWS, depth), bf16),
-            pltpu.VMEM((depth, tokens), bf16),
             pltpu.VMEM((CHUNKS, tokens, width), bf16),
             pltpu.VMEM((CHUNKS, half, width), bf16),
             pltpu.VMEM((CHUNKS, half, width), bf16),
@@ -275,7 +311,6 @@
             pltpu.VMEM((CHUNKS, 2, ROWS, width), bf16),
             pltpu.VMEM((CHUNKS, 2, 2, ROWS, width), bf16),
             pltpu.VMEM((CHUNKS, 2, ROWS, width), bf16),
-            pltpu.VMEM((tokens, depth), f32),
             dma((2,)),
             per_chunk,
             dma((10,)),
@@ -292,7 +327,7 @@
             dma,
             per_chunk,
         ],
-        compiler_params=pltpu.CompilerParams(collective_id=0, has_side_effects=True, vmem_limit_bytes=52 << 20),
+        compiler_params=pltpu.CompilerParams(collective_id=0, has_side_effects=True, vmem_limit_bytes=50 << 20),
         cost_estimate=pl.CostEstimate(flops=6 * tokens * depth * model, bytes_accessed=14 << 20, transcendentals=0),
         name="relay_section",
     )(heads_out.reshape(blocked), weight, incoming[0], parked.reshape(blocked))
@@ -303,10 +338,10 @@
             jax.ShapeDtypeStruct(blocked, bf16),
             jax.ShapeDtypeStruct((depth, model), bf16),
         ),
-        in_specs=[pl.BlockSpec(memory_space=pltpu.VMEM)] * 3,
+        in_specs=[pl.BlockSpec(memory_space=pltpu.VMEM)] * 6,
         out_specs=[pl.BlockSpec(memory_space=pl.ANY)] * 3,
-        scratch_shapes=[dma((3,))],
-        compiler_params=pltpu.CompilerParams(vmem_limit_bytes=2 << 20),
+        scratch_shapes=[pltpu.VMEM((2, 8, ROWS, depth), bf16), pltpu.VMEM((depth, width), bf16), dma((4,))],
+        compiler_params=pltpu.CompilerParams(vmem_limit_bytes=12 << 20),
         name="publish",
     )(*(pltpu.with_memory_space_constraint(out, pltpu.VMEM) for out in outs))
     return activation[None], heads_gradient.reshape(1, tokens, depth), weight_gradient[None]

time: 123 us -> 121 us (0.984)
  Pallas kernels: 122 us -> 120 us
    pallas_call x1, Pallas kernels: 120 us -> 117 us  [section_step(): pl.pallas_call(kernel, out_shape=(pltpu.VMEM((CHUNKS, ROWS, width), bf16)...]
where the time goes in v3:
time: 121 us
  Pallas kernels  120 us (99%)
    pallas_call x1, Pallas kernels, section_step(): pl.pallas_call(kernel, out_shape=(pltpu.VMEM((CHUNKS, ROWS, width), bf16)...  117 us
    pallas_call x1, Pallas kernels, section_step(): pl.pallas_call(publish, out_shape=(jax.ShapeDtypeStruct((ROWS, model), bf...  3.2 us

profile of v3, /device:TPU:1, one launch (start us, length us, event | category | flops | bytes accessed | tf_op | source)
XLA Modules:
  0.0 120.9 jit_solution(1111860853749161930)
XLA Ops:
  0.6 117.1 %relay_section.1 = (bf16[12,64,512]{2,1,0:T(8,128)(2,1)S(1)}, f32[1024,384]{1,0:T(8,128)S(1)}, bf16[384,1024]{1,0:T(8,128)(2,1)S(1)}, bf16[11,384,512]{2,1,0:T(8...) custom-call(bf16[8,2,64,384]{3,2,1,0:T(8,128)(2,1)} %bitcast.9, bf16[384,6144]{1,0:T(8,128)(2,1)} %bitcast.7, ...), custom_call_target="tpu_custom_call" | custom-call | flops 14495514624 | bytes 14680064 | tf_op jit(solution)/shard_map/relay_section/pallas_call | solution.py:291
  117.7 3.2 %publish.1 = (bf16[64,6144]{1,0:T(8,128)(2,1)}, bf16[8,2,64,384]{3,2,1,0:T(8,128)(2,1)}, bf16[384,6144]{1,0:T(8,128)(2,1)}) custom-call(bf16[12,64,512]{2,1,0:T(8,128)(2,1)S(1)} %get-tuple-element.12.act_v, f32[1024,384]{1,0:T(8,128)S(1)} %get-tuple-element.13.total, bf16[384,1024]{1,0:T(8,128)(2,1)S(1)} %get-tuple-element.14.turned_v, ...), custom_call_target="tpu_custom_call" | custom-call | tf_op jit(solution)/shard_map/publish/pallas_call | solution.py:334

commit v4 on v3

--- a/solution.py
+++ b/solution.py
@@ -12,12 +12,12 @@
 ROWS = 64
 STAGES = {
     "launch": -4,
-    "share": -1,
-    "combine": 0,
     "relay": 2,
     "reduce": 4,
     "spread": 2,
     "forward": 4,
+    "share": -1,
+    "combine": 0,
     "pair": 6,
     "multiply": 7,
     "finish": 9,

time: 121 us -> 121 us (level)
  no operation moved by 1% of the time
where the time goes in v4:
time: 121 us
  Pallas kernels  120 us (99%)
    pallas_call x1, Pallas kernels, section_step(): pl.pallas_call(kernel, out_shape=(pltpu.VMEM((CHUNKS, ROWS, width), bf16)...  117 us
    pallas_call x1, Pallas kernels, section_step(): pl.pallas_call(publish, out_shape=(jax.ShapeDtypeStruct((ROWS, model), bf...  3.19 us

profile of v4, /device:TPU:1, one launch (start us, length us, event | category | flops | bytes accessed | tf_op | source)
XLA Modules:
  0.0 120.9 jit_solution(5768782805724171422)
XLA Ops:
  0.6 117.1 %relay_section.1 = (bf16[12,64,512]{2,1,0:T(8,128)(2,1)S(1)}, f32[1024,384]{1,0:T(8,128)S(1)}, bf16[384,1024]{1,0:T(8,128)(2,1)S(1)}, bf16[11,384,512]{2,1,0:T(8...) custom-call(bf16[8,2,64,384]{3,2,1,0:T(8,128)(2,1)} %bitcast.9, bf16[384,6144]{1,0:T(8,128)(2,1)} %bitcast.7, ...), custom_call_target="tpu_custom_call" | custom-call | flops 14495514624 | bytes 14680064 | tf_op jit(solution)/shard_map/relay_section/pallas_call | solution.py:291
  117.7 3.2 %publish.1 = (bf16[64,6144]{1,0:T(8,128)(2,1)}, bf16[8,2,64,384]{3,2,1,0:T(8,128)(2,1)}, bf16[384,6144]{1,0:T(8,128)(2,1)}) custom-call(bf16[12,64,512]{2,1,0:T(8,128)(2,1)S(1)} %get-tuple-element.12.act_v, f32[1024,384]{1,0:T(8,128)S(1)} %get-tuple-element.13.total, bf16[384,1024]{1,0:T(8,128)(2,1)S(1)} %get-tuple-element.14.turned_v, ...), custom_call_target="tpu_custom_call" | custom-call | tf_op jit(solution)/shard_map/publish/pallas_call | solution.py:334
